TPU v7x, 256 devices: a whole 4x4x8 slice. The times are simulated.
256 devices in a mesh: dp: 32 (over y, z), tensor: 8 (over x, core).
Axes of the slice: x: 4, y: 4, z: 8, core: 2. Of those that a mesh axis runs over, the one named last changes fastest.
Arguments:
- layer_inputs: bfloat16 [4096, 4, 1024], P('dp', None, 'tensor'), may hold values from -125 to 125
- output_grads: bfloat16 [4096, 10240], P('dp'), may hold values from -0.0109375 to 0.0109375
- left_stats: float32 [32, 2, 1024, 1024], P('dp', None, 'tensor'), may hold values from -6 to 6
- right_stats: float32 [32, 2, 1024, 1024], P('dp', None, 'tensor'), may hold values from -6 to 6
- left_roots: bfloat16 [32, 2, 1024, 1024], P('dp', None, 'tensor'), may hold values from -0.2 to 7.2
- right_roots: bfloat16 [32, 2, 1024, 1024], P('dp'), may hold values from -0.2 to 2.2
- owner_blocks: int32 [32, 2], replicated, may hold values from -1 to 39, as said below
- block_counts: int32 [32], replicated, may hold values from 0 to 2, as said below
Outputs:
- new_left: float32 [32, 2, 1024, 1024], P('dp', None, 'tensor')
- new_right: float32 [32, 2, 1024, 1024], P('dp', None, 'tensor')
- grafted_update: bfloat16 [1024, 4, 10240], P(('tensor', 'dp'))
Inputs may be any that keep to these rules, and one draw needn't show every extreme that they name: `owner_blocks`: row o lists, in slots 0 to block_counts[o] - 1, the blocks that dp index o owns, numbered i * 10 + j for block row i and block column j; every block is listed exactly once over all rows; the other slots hold -1; some owner lists 2 blocks. `block_counts`: number of blocks of each owner; they sum to 40.
All inputs are finite; a program needn't handle non-finite values.
Results may differ from a plain program's by a relative error of at most 0.025.
Values may be sent and summed in bfloat16 or wider, within the bound.
A program may use at most 128 MiB of HBM per device.

v0:
```python
import jax
import jax.numpy as jnp
from jax import lax
from jax.sharding import PartitionSpec as P

decay_rate = 0.99
epsilon = 1e-06


def body(
    layer_inputs,
    output_grads,
    left_stats,
    right_stats,
    left_roots,
    right_roots,
    owner_blocks,
    block_counts,
):
    block_width = left_roots.shape[-1]
    slot_total = left_stats.shape[1]
    tensor_rows = left_stats.shape[2]
    groups = lax.axis_size("dp")
    device_rows = tensor_rows // groups
    row_blocks = layer_inputs.shape[1]
    columns = output_grads.shape[1]
    block_total = row_blocks * (columns // block_width)
    slot_iota = jnp.arange(slot_total, dtype=jnp.int32)
    every_live = slot_iota[None, :] < block_counts[:, None]
    every_block = jnp.clip(owner_blocks, 0, block_total - 1)
    partials = jnp.einsum(
        "tik,tc->kic", layer_inputs, output_grads, preferred_element_type=jnp.float32
    )
    partials = partials.reshape(tensor_rows, block_total, block_width)
    owners = tensor_rows * lax.axis_size("dp") // tensor_rows
    listed = every_block.reshape(-1)
    alive = every_live.reshape(-1)
    chosen = jnp.take(partials, listed, axis=1)
    chosen = jnp.where(alive[None, :, None], chosen, 0.0)
    chosen = chosen.reshape(tensor_rows, owners, slot_total, block_width)
    summed = lax.psum_scatter(
        jnp.transpose(chosen, (1, 0, 2, 3))
        .reshape(tensor_rows * lax.axis_size("dp"), slot_total, block_width)
        .astype(jnp.bfloat16),
        "dp",
        scatter_dimension=0,
        tiled=True,
    )
    tensor_index = lax.axis_index("tensor")
    full_blocks = lax.all_gather(summed, "tensor", axis=0, tiled=True)
    left_gram = jnp.einsum("asc,qsc->saq", summed, full_blocks, preferred_element_type=jnp.float32)
    column_part = lax.dynamic_slice_in_dim(full_blocks, tensor_index * tensor_rows, tensor_rows, 2)
    right_gram = jnp.einsum(
        "rsa,rsc->sac", column_part, full_blocks, preferred_element_type=jnp.float32
    )
    new_left = decay_rate * left_stats[0] + (1.0 - decay_rate) * left_gram
    new_right = decay_rate * right_stats[0] + (1.0 - decay_rate) * right_gram
    applied = jnp.einsum(
        "sar,rsc->sac", left_roots[0], full_blocks, preferred_element_type=jnp.float32
    ).astype(jnp.bfloat16)
    precond = jnp.einsum(
        "sac,scd->asd", applied, right_roots[0], preferred_element_type=jnp.float32
    )
    grad_sq = jnp.sum(jnp.square(summed.astype(jnp.float32)), axis=(0, 2))
    prec_sq = jnp.sum(jnp.square(precond), axis=(0, 2))
    grad_sq, prec_sq = lax.psum((grad_sq, prec_sq), "tensor")
    graft_scale = jnp.sqrt(grad_sq) * lax.rsqrt(prec_sq + epsilon)
    grafted = (precond * graft_scale[None, :, None]).astype(jnp.bfloat16)
    returned = lax.all_to_all(
        grafted.reshape(groups, device_rows, slot_total, block_width),
        "dp",
        split_axis=0,
        concat_axis=0,
        tiled=True,
    )
    selector = (
        every_block[:, :, None] == jnp.arange(block_total, dtype=jnp.int32)[None, None, :]
    ) & every_live[:, :, None]
    placed = jnp.einsum(
        "orsc,osb->rbc", returned, selector.astype(jnp.bfloat16), preferred_element_type=jnp.float32
    )
    update = placed.astype(jnp.bfloat16).reshape(device_rows, row_blocks, columns)
    return (new_left[None], new_right[None], update)


def solution(mesh):
    placed = (
        P("dp", None, "tensor"),
        P("dp", None),
        P("dp", None, "tensor", None),
        P("dp", None, "tensor", None),
        P("dp", None, "tensor", None),
        P("dp", None, None, None),
        P(),
        P(),
    )
    return jax.shard_map(
        body,
        mesh=mesh,
        in_specs=placed,
        out_specs=(
            P("dp", None, "tensor", None),
            P("dp", None, "tensor", None),
            P(("tensor", "dp"), None, None),
        ),
        check_vma=False,
    )
```

profile of v0, /device:TPU:1, one launch (start us, length us, event | category | flops | bytes accessed | tf_op | source)
XLA Modules:
  0.0 399.9 jit_solution(15104308494538079885)
XLA Ops:
  7.2 0.0 copy-start
  7.2 0.0 reduce-scatter.2.cloned.1.call-start
  7.2 0.8 broadcast_clamp_fusion
  8.1 0.1 copy.25
  8.2 0.1 reshape.97
  8.3 0.6 copy-done
  8.9 6.4 %fusion.2 = bf16[10240,4,128]{2,0,1:T(8,128)(2,1)} fusion(bf16[128,10240]{1,0:T(8,128)(2,1)S(1)} %copy-done, bf16[128,4,128]{2,1,0:T(4,128)(2,1)} %param.8), kind=kOutput, calls=%fused_computation.4 | convolution fusion | flops 1342177280 | bytes 13238272 | tf_op jit(solution)/shard_map/tik,tc->kic/dot_general | solution.py:31
  15.4 11.5 %gather_fusion = bf16[64,128,1024]{1,2,0:T(8,128)(2,1)} fusion(bf16[128,40,1024]{0,2,1:T(8,128)(2,1)} %bitcast.52, s32[1024]{0:T(1024)S(1)} %pad_clamp_fusion), kind=kCustom, calls=%fused_computation | custom fusion | bytes 33554688 | tf_op jit(solution)/shard_map/jit(_take)/gather | solution.py:38
  26.8 0.0 copy-start.5
  26.8 0.0 copy-start.6
  26.8 21.3 %copy.26 = bf16[128,32,2,1024]{3,0,1,2:T(8,128)(2,1)} copy(bf16[128,32,2,1024]{0,3,2,1:T(8,128)(2,1)} %bitcast.54) | data formatting | bytes 33554432 | tf_op jit(solution)/shard_map/jit(_take)/gather | solution.py:38
  48.1 0.0 copy-done.5
  48.1 0.0 copy-done.6
  48.1 15.9 %select_convert_fusion = bf16[128,32,2,1024]{3,0,1,2:T(8,128)(2,1)} fusion(bf16[128,32,2,1024]{3,0,1,2:T(8,128)(2,1)} %copy.26, pred[32,2]{0,1:T(4,128)(4,1)S(1)} %get-tuple-element.7, pred[32,2]{0,1:T(4,128)(4,1)S(1)} %get-tuple-element.8), kind=kLoop, calls=%fused_computation.1 | loop fusion | flops 16777216 | bytes 33554560 | tf_op jit(solution)/shard_map/convert_element_type | solution.py:44
  64.0 0.0 copy-start.4
  64.0 0.0 reduce-scatter.2.cloned.1.call-update
  64.0 0.0 all-gather.2.cloned.1.call-start
  64.1 244.2 %reduce-scatter.2.cloned.1.call-done = bf16[128,2,1024]{2,0,1:T(8,128)(2,1)} async-done(((bf16[4096,2,1024]{2,0,1:T(8,128)(2,1)}), bf16[128,2,1024]{2,0,1:T(8,128)(2,1)}) %reduce-scatter.2.cloned.1.call-update) | async-done | bytes 524304 | tf_op jit(solution)/shard_map/reduce_scatter | solution.py:41
  308.3 0.0 all-gather.2.cloned.1.call-update
  308.4 1.3 multiply_reduce_fusion.1
  309.7 38.1 %all-gather.2.cloned.1.call-done = bf16[1024,2,1024]{2,0,1:T(8,128)(2,1)} async-done(((bf16[128,2,1024]{2,0,1:T(8,128)(2,1)}), bf16[1024,2,1024]{2,0,1:T(8,128)(2,1)}) %all-gather.2.cloned.1.call-update) | async-done | bytes 4194320 | tf_op jit(solution)/shard_map/all_gather | solution.py:50
  347.8 0.0 copy-done.4
  347.8 5.7 %multiply_reduce_fusion = (f32[2]{0:T(128)S(1)}, f32[2,128,1024]{2,1,0:T(8,128)S(1)}) fusion(bf16[1,2,1024,1024]{3,2,1,0:T(8,128)(2,1)} %param.13, bf16[1024,2,1024]{2,0,1:T(8,128)(2,1)} %all-gather.2.cloned.1.call-done, bf16[1,2,128,1024]{3,2,1,0:T(8,128)(2,1)S(1)} %copy-done.4), kind=kOutput, calls=%fused_computation.17 | convolution fusion | flops 1074528256 | bytes 9961480 | tf_op jit(solution)/shard_map/sac,scd->asd/dot_general | solution.py:61
  353.5 12.0 %all-reduce = (f32[2]{0:T(128)S(1)}, f32[2]{0:T(128)S(1)}) all-reduce(f32[2]{0:T(128)S(1)} %get-tuple-element.5, f32[2]{0:T(128)S(1)} %multiply_reduce_fusion.1), channel_id=1, replica_groups=mesh['dp'=32,'tensor'=8] {'tensor'}, use_global_device_ids=true, to_apply=%region_4.5 | all-reduce | flops 4 | bytes 32 | tf_op jit(solution)/shard_map/psum | solution.py:66
  365.5 0.2 fusion.10
  365.7 1.3 copy.38
  367.0 0.0 copy-start.3
  367.0 9.8 %all-to-all-start = ((bf16[32,4,2,1024]{3,2,1,0:T(2,128)(2,1)}), bf16[32,4,2,1024]{3,2,1,0:T(2,128)(2,1)}, u32[]{:S(2)}, u32[]{:S(2)}) async-start(bf16[32,4,2,1024]{3,2,1,0:T(2,128)(2,1)} %bitcast.16), calls=%async_computation.1 | async-start | bytes 1048576 | tf_op jit(solution)/shard_map/all_to_all | solution.py:69
  376.9 0.0 copy-start.2
  376.9 0.0 copy-start.1
  376.9 4.7 %fusion.5 = f32[1,2,128,1024]{3,2,1,0:T(8,128)} fusion(bf16[1024,2,1024]{2,0,1:T(8,128)(2,1)} %all-gather.2.cloned.1.call-done, f32[1,2,128,1024]{3,2,1,0:T(8,128)} %param.11, s32[]{:T(128)S(6)} %select_n.34), kind=kOutput, calls=%fused_computation.8 | convolution fusion | flops 537657344 | bytes 6815748 | tf_op jit(solution)/shard_map/rsa,rsc->sac/dot_general | solution.py:53
  381.6 0.0 copy-done.3
  381.6 0.0 copy-done.2
  381.6 3.8 fusion.7
  385.3 5.1 %all-to-all-done = bf16[32,4,2,1024]{3,2,1,0:T(2,128)(2,1)} async-done(((bf16[32,4,2,1024]{3,2,1,0:T(2,128)(2,1)}), bf16[32,4,2,1024]{3,2,1,0:T(2,128)(2,1)}, u32[]{:S(2)}, u32[]{:S(2)}) %all-to-all-start) | async-done | bytes 524320 | tf_op jit(solution)/shard_map/all_to_all | solution.py:69
  390.5 1.5 fusion.9
  392.0 1.1 reshape.99
  393.1 0.0 copy-done.1
  (4 shorter events, 0.0 us)
Async XLA Ops:
  7.2 1.8 copy-start
  7.2 301.2 %reduce-scatter.2.cloned.1.call-start = ((), (), s32[]{:S(2)}) async-start(), calls=%async_computation.2 | async-start | bytes 17301504 | tf_op jit(solution)/shard_map/reduce_scatter | solution.py:41
  26.8 21.3 %copy-start.5 = (s32[32,2]{0,1:T(2,128)S(1)}, s32[32,2]{0,1:T(2,128)}, u32[]{:S(2)}) copy-start(s32[32,2]{0,1:T(2,128)} %param.14) | copy-start | bytes 772
  26.8 21.3 %copy-start.6 = (s32[32]{0:T(128)S(1)}, s32[32]{0:T(128)}, u32[]{:S(2)}) copy-start(s32[32]{0:T(128)} %param.15) | copy-start | bytes 388
  64.0 283.7 %copy-start.4 = (bf16[1,2,128,1024]{3,2,1,0:T(8,128)(2,1)S(1)}, bf16[1,2,128,1024]{3,2,1,0:T(8,128)(2,1)}, u32[]{:S(2)}) copy-start(bf16[1,2,128,1024]{3,2,1,0:T(8,128)(2,1)} %param.12) | copy-start | bytes 1572868
  64.0 283.7 %all-gather.2.cloned.1.call-start = ((), (), s32[]{:S(2)}) async-start(), calls=%async_computation.3 | async-start | bytes 4718592 | tf_op jit(solution)/shard_map/all_gather | solution.py:50
  367.0 14.5 %copy-start.3 = (bf16[128,2,1024]{2,0,1:T(8,128)(2,1)S(1)}, bf16[128,2,1024]{2,0,1:T(8,128)(2,1)}, u32[]{:S(2)}) copy-start(bf16[128,2,1024]{2,0,1:T(8,128)(2,1)} %reduce-scatter.2.cloned.1.call-done) | copy-start | bytes 1572868
  367.0 23.4 %all-to-all-start = ((bf16[32,4,2,1024]{3,2,1,0:T(2,128)(2,1)}), bf16[32,4,2,1024]{3,2,1,0:T(2,128)(2,1)}, u32[]{:S(2)}, u32[]{:S(2)}) async-start(bf16[32,4,2,1024]{3,2,1,0:T(2,128)(2,1)} %bitcast.16), calls=%async_computation.1 | async-start | bytes 1048576 | tf_op jit(solution)/shard_map/all_to_all | solution.py:69
  376.9 4.7 %copy-start.2 = (bf16[1024,2,1024]{2,0,1:T(8,128)(2,1)S(1)}, bf16[1024,2,1024]{2,0,1:T(8,128)(2,1)}, u32[]{:S(2)}) copy-start(bf16[1024,2,1024]{2,0,1:T(8,128)(2,1)} %all-gather.2.cloned.1.call-done) | copy-start | bytes 12582916
  376.9 16.2 %copy-start.1 = (bf16[128,10240]{1,0:T(8,128)(2,1)S(1)}, bf16[128,10240]{1,0:T(8,128)(2,1)}, u32[]{:S(2)}) copy-start(bf16[128,10240]{1,0:T(8,128)(2,1)} %param.9) | copy-start | bytes 7864324
Sparse Core Ops, SparseCore 0:
  64.2 244.1 reduce-scatter.1
  310.2 37.5 all-gather.1
where the time goes:
time: 404 us; the launch traced here: 400 us
  waiting for transfers between devices  288 us (71%)
  local copies, waits for them, and re-layouts  36 us (9%)
  matrix products  22.1 us (5%)
  other arithmetic  18.2 us (5%)
  between operations  14.1 us (3%)
  blocking collectives  12 us (3%)
  starting transfers between devices  9.91 us (2%)
    reduce_scatter x1, waiting for transfers between devices, body(): lax.psum_scatter(jnp.transpose(chosen, (1, 0, 2, 3)).reshape(tensor_rows...  244 us
    all_gather x1, waiting for transfers between devices, body(): full_blocks = lax.all_gather(summed, 'tensor', axis=0, tiled=True)  38.1 us
    gather x2, local copies, waits for them, and re-layouts, body(): chosen = jnp.take(partials, listed, axis=1)  32.7 us
    convert_element_type x1, other arithmetic, body(): summed = lax.psum_scatter(jnp.transpose(chosen, (1, 0, 2, 3)).reshape(ten...  15.9 us
    psum x1, blocking collectives, body(): grad_sq, prec_sq = lax.psum((grad_sq, prec_sq), 'tensor')  12 us
    all_to_all x1, starting transfers between devices, body(): lax.all_to_all(grafted.reshape(groups, device_rows, slot_total, block_wid...  9.83 us
  transfers between devices with their start and end apart: 3, of which 3 were waited for; matrix products, arithmetic and copies ran while one was open for 2% of the time, Pallas kernels for 0%

commit v1 on v0

v1 whole, which is shorter than its diff:
```python
import functools

import jax
import jax.numpy as jnp
from jax import lax
from jax.experimental import pallas as pl
from jax.experimental.pallas import tpu as pltpu
from jax.sharding import PartitionSpec as P

decay_rate = 0.99
epsilon = 1e-06

NY, NZ = 4, 8
NX = 4
N_DP = NY * NZ
N_T = NX * 2
BL = 1024
ROWS = 128
NRB, NCB = 4, 10
NB = NRB * NCB
TOK = 128
CW = BL // N_DP
GROWS = NCB * CW
GX = GROWS // NX
SPAN = 3
TA = 80
TAH = 48
TB = TOK - TA
TBH = 32
HALF = N_DP // 2

MESH = pl.DeviceIdType.MESH


def remote(src, dst, send_sem, recv_sem, device):
    return pltpu.make_async_remote_copy(
        src_ref=src,
        dst_ref=dst,
        send_sem=send_sem,
        recv_sem=recv_sem,
        device_id=device,
        device_id_type=MESH,
    )


def await_bytes(ref, sem):
    pltpu.make_async_copy(ref, ref, sem).wait()


def kernel(
    x_hbm,
    g_hbm,
    ls_hbm,
    rs_hbm,
    lr_hbm,
    rr_hbm,
    send_idx,
    slot_of,
    nl_hbm,
    nr_hbm,
    up_hbm,
    xall,
    gin,
    gsend,
    gt,
    acc,
    tiles,
    sbuf,
    bt,
    lhs,
    rr,
    ls,
    rs,
    norms,
    pbuf,
    rv,
    up,
    load_sem,
    out_sem,
    xs_sem,
    az_sem,
    ay_sem,
    by_sem,
    bz_sem,
    gs_sem,
    gr_sem,
    gx_sem,
    gc_sem,
    ss_sem,
    sr_sem,
    bx_sem,
    bc_sem,
    nsend_sem,
    nr_sem,
    ps_sem,
    pr_sem,
):
    g = lax.axis_index("dp")
    t = lax.axis_index("tensor")
    y, z = g // NZ, g % NZ
    x, core = t // 2, t % 2
    yp, ym = (y + 1) % NY, (y + NY - 1) % NY
    zp, zm = (z + 1) % NZ, (z + NZ - 1) % NZ
    xp, xm = (x + 1) % NX, (x + NX - 1) % NX
    dev_yp, dev_ym = (yp * NZ + z, t), (ym * NZ + z, t)
    dev_zp, dev_zm = (y * NZ + zp, t), (y * NZ + zm, t)
    dev_xp, dev_xm = (g, xp * 2 + core), (g, xm * 2 + core)
    dev_c = (g, x * 2 + 1 - core)
    lane_t = pl.multiple_of(t * ROWS, ROWS)

    own_x = pltpu.make_async_copy(x_hbm, xall.at[y, z], load_sem.at[0])
    own_x.start()
    j0 = (5 * x) // 2
    load_g = pltpu.make_async_copy(
        g_hbm.at[:, pl.ds(pl.multiple_of(j0 * BL, BL), SPAN * BL)], gin, load_sem.at[1]
    )
    load_g.start()
    later = [
        pltpu.make_async_copy(lr_hbm, lhs.at[:, pl.ds(ROWS, ROWS)], load_sem.at[2]),
        pltpu.make_async_copy(rr_hbm, rr, load_sem.at[3]),
        pltpu.make_async_copy(ls_hbm, ls, load_sem.at[4]),
        pltpu.make_async_copy(rs_hbm, rs, load_sem.at[5]),
    ]
    for copy in later:
        copy.start()

    barrier = pltpu.get_barrier_semaphore()

    def greet_dp(d, carry):
        pl.semaphore_signal(barrier, inc=1, device_id=((g + d) % N_DP, t), device_id_type=MESH)
        return carry

    def greet_tensor(d, carry):
        pl.semaphore_signal(barrier, inc=1, device_id=(g, (t + d) % N_T), device_id_type=MESH)
        return carry

    lax.fori_loop(1, N_DP, greet_dp, 0)
    lax.fori_loop(1, N_T, greet_tensor, 0)
    pl.semaphore_wait(barrier, N_DP + N_T - 2)

    def az(k, right):
        zs = (z + NZ - k) % NZ if right else (z + k) % NZ
        if k < 3:
            rows = pl.ds(0, TA)
        else:
            rows = pl.ds(0, TAH) if right else pl.ds(TAH, TA - TAH)
        ref = xall.at[y, zs, rows]
        n = k * 2 + (0 if right else 1)
        return remote(ref, ref, xs_sem.at[n], az_sem.at[n], dev_zp if right else dev_zm)

    def by(k, right):
        if k == 0:
            ys, rows = y, pl.ds(TA, TB)
        elif right:
            ys, rows = ym, pl.ds(TA, TBH)
        else:
            ys, rows = yp, pl.ds(TA + TBH, TB - TBH)
        ref = xall.at[ys, z, rows]
        n = k * 2 + (0 if right else 1)
        return remote(ref, ref, xs_sem.at[8 + n], by_sem.at[n], dev_yp if right else dev_ym)

    def bz(k, right):
        zs = (z + NZ - k) % NZ if right else (z + k) % NZ
        if k < 3:
            rows = pl.ds(TA, TB)
        else:
            rows = pl.ds(TA, TBH) if right else pl.ds(TA + TBH, TB - TBH)
        ref = xall.at[:, zs, rows]
        n = k * 2 + (0 if right else 1)
        return remote(ref, ref, xs_sem.at[12 + n], bz_sem.at[n], dev_zp if right else dev_zm)

    def ay(k, right):
        if k == 0:
            ys, zs = y, pl.ds(0, NZ)
        elif right:
            ys, zs = ym, pl.ds(0, NZ // 2)
        else:
            ys, zs = yp, pl.ds(NZ // 2, NZ // 2)
        ref = xall.at[ys, zs, pl.ds(0, TA)]
        n = k * 2 + (0 if right else 1)
        return remote(ref, ref, xs_sem.at[20 + n], ay_sem.at[n], dev_yp if right else dev_ym)

    own_x.wait()
    for right in (True, False):
        az(0, right).start()
        by(0, right).start()

    load_g.wait()
    offset = pl.multiple_of(((5 * x) % 2) * 16, 16)
    gx_rows = pl.ds(pl.multiple_of(x * GX, 16), GX)
    sends_g = core == y // 2

    @pl.when(sends_g)
    def _():
        for j in range(SPAN):
            block = gin[:, j * BL : (j + 1) * BL].T
            gsend[:, j * CW : (j + 1) * CW, :] = block.reshape(N_DP, CW, TOK)

        lanes = pl.ds(pl.multiple_of(g * TOK, TOK), TOK)
        own = pltpu.make_async_copy(
            gsend.at[g, pl.ds(offset, GX)], gt.at[gx_rows, lanes], gr_sem
        )
        own.start()

        def send_g(d, carry):
            to = (g + d) % N_DP
            remote(
                gsend.at[to, pl.ds(offset, GX)], gt.at[gx_rows, lanes], gs_sem, gr_sem, (to, t)
            ).start()
            return carry

        lax.fori_loop(1, N_DP, send_g, 0)

    for k in range(1, 4):
        for right in (True, False):
            az(k - 1, right).wait_recv()
            az(k, right).start()
        if k == 1:
            for right in (True, False):
                by(0, right).wait_recv()
                by(1, right).start()
    for right in (True, False):
        by(1, right).wait_recv()
    for right in (True, False):
        bz(0, right).start()
    for right in (True, False):
        az(3, right).wait_recv()
    for right in (True, False):
        ay(0, right).start()

    half_lanes = pl.ds(pl.multiple_of(core * HALF * TOK, HALF * TOK), HALF * TOK)
    await_bytes(gt.at[gx_rows, half_lanes], gr_sem)

    def gxc(k, right):
        if k == 0:
            start, size = x * GX, GX
        elif right:
            start, size = xm * GX, 48
        else:
            start, size = xp * GX + 48, 32
        ref = gt.at[pl.ds(pl.multiple_of(start, 16), size), half_lanes]
        n = k * 2 + (0 if right else 1)
        return remote(ref, ref, xs_sem.at[24 + n], gx_sem.at[n], dev_xp if right else dev_xm)

    for right in (True, False):
        gxc(0, right).start()
    for right in (True, False):
        bz(0, right).wait_recv()
        bz(1, right).start()
    for right in (True, False):
        gxc(0, right).wait_recv()
        gxc(1, right).start()
    for right in (True, False):
        bz(1, right).wait_recv()
        bz(2, right).start()
    for right in (True, False):
        ay(0, right).wait_recv()
        ay(1, right).start()
    for right in (True, False):
        gxc(1, right).wait_recv()
    gcc = remote(
        gt.at[:, half_lanes], gt.at[:, half_lanes], xs_sem.at[28], gc_sem, dev_c
    )
    gcc.start()
    for right in (True, False):
        bz(2, right).wait_recv()
        bz(3, right).start()
    gcc.wait_recv()
    for right in (True, False):
        ay(1, right).wait_recv()
    for right in (True, False):
        bz(3, right).wait_recv()

    acc[...] = jnp.zeros_like(acc)
    depth = 4 * TOK

    def add_tokens(n, carry):
        lanes = pl.ds(pl.multiple_of(n * depth, depth), depth)
        part = xall[n // 2, pl.ds((n % 2) * 4, 4)].reshape(depth, NRB * ROWS)
        acc[...] += jnp.dot(gt[:, lanes], part, preferred_element_type=jnp.float32)
        return carry

    lax.fori_loop(0, N_DP * TOK // depth, add_tokens, 0)
    for i in range(NRB):
        for j in range(NCB):
            tiles[i * NCB + j] = acc[
                j * CW : (j + 1) * CW, i * ROWS : (i + 1) * ROWS
            ].astype(jnp.bfloat16)
    tiles[NB] = jnp.zeros((CW, ROWS), jnp.bfloat16)

    bt_rows = pl.ds(pl.multiple_of(g * CW, CW), CW)
    bt_lanes = pl.ds(lane_t, ROWS)
    for s in range(2):

        def send_block(d, carry):
            to = (g + d) % N_DP
            sbuf[s, to] = tiles[send_idx[to * 2 + s]]
            remote(
                sbuf.at[s, to], bt.at[s, bt_rows, bt_lanes], ss_sem.at[s], sr_sem.at[s], (to, t)
            ).start()
            return carry

        sbuf[s, g] = tiles[send_idx[g * 2 + s]]
        pltpu.make_async_copy(sbuf.at[s, g], bt.at[s, bt_rows, bt_lanes], sr_sem.at[s]).start()
        lax.fori_loop(1, N_DP, send_block, 0)

    def lanes_of(xs, cs):
        return pl.ds(pl.multiple_of((xs * 2 + cs) * ROWS, ROWS), ROWS)

    def bxc(s, k, right):
        if k == 0:
            xs, rows = x, pl.ds(0, BL)
        elif right:
            xs, rows = xm, pl.ds(0, BL // 2)
        else:
            xs, rows = xp, pl.ds(BL // 2, BL // 2)
        ref = bt.at[s, rows, lanes_of(xs, core)]
        n = s * 4 + k * 2 + (0 if right else 1)
        return remote(ref, ref, xs_sem.at[29 + n], bx_sem.at[n], dev_xp if right else dev_xm)

    def bcc(s, step, sending=True):
        xs = (x + NX - step) % NX
        ref = bt.at[s, :, lanes_of(xs, core if sending else 1 - core)]
        n = s * 4 + step
        return remote(ref, ref, xs_sem.at[37 + n], bc_sem.at[n], dev_c)

    def gather_start(s):
        await_bytes(bt.at[s, :, bt_lanes], sr_sem.at[s])
        for right in (True, False):
            bxc(s, 0, right).start()
        bcc(s, 0).start()

    def gather_middle(s):
        bxc(s, 0, True).wait_recv()
        bxc(s, 1, True).start()
        bcc(s, 1).start()
        bxc(s, 0, False).wait_recv()
        bxc(s, 1, False).start()
        bcc(s, 3).start()

    def gather_end(s):
        for right in (True, False):
            bxc(s, 1, right).wait_recv()
        bcc(s, 2).start()
        for step in (0, 1, 3, 2):
            bcc(s, step, False).wait_recv()

    def norm_copy(s, d):
        ref = norms.at[s, t]
        return remote(ref, ref, nsend_sem.at[s], nr_sem.at[s, d], (g, (t + d) % N_T))

    def precondition(s):
        lhs[s, 0:ROWS] = bt[s, pl.ds(lane_t, ROWS), :]
        both = lax.dot_general(
            lhs[s], bt[s], (((1,), (1,)), ((), ())), preferred_element_type=jnp.float32
        )
        rs[s] = decay_rate * rs[s] + (1.0 - decay_rate) * both[0:ROWS]
        pltpu.make_async_copy(rs.at[s], nr_hbm.at[s], out_sem.at[s]).start()
        applied = both[ROWS:].astype(jnp.bfloat16)
        precond = jnp.dot(applied, rr[s], preferred_element_type=jnp.float32)
        own = bt[s, :, bt_lanes].astype(jnp.float32)
        norms[s, t, 0:8] = jnp.sum((own * own).reshape(-1, 8, ROWS), axis=0)
        squares = precond * precond
        folded = jnp.sum(squares.reshape(-1, 8, BL), axis=0)
        total = folded[:, 0:ROWS]
        for m in range(1, BL // ROWS):
            total = total + folded[:, m * ROWS : (m + 1) * ROWS]
        norms[s, t, 8:16] = total
        for d in range(1, N_T):
            norm_copy(s, d).start()
        for d in range(1, N_T):
            norm_copy(s, d).wait_recv()
        sums = jnp.sum(norms[s], axis=0)
        grad_sq = jnp.sum(sums[0:8], keepdims=True)
        prec_sq = jnp.sum(sums[8:16], keepdims=True)
        scale = jnp.sqrt(grad_sq) * lax.rsqrt(prec_sq + epsilon)
        grafted = precond * scale
        pbuf[s] = grafted.reshape(ROWS, 8, ROWS).reshape(N_DP, 32, ROWS).astype(jnp.bfloat16)
        pltpu.make_async_copy(pbuf.at[s, g], rv.at[s, g], pr_sem.at[s]).start()

        def send_back(d, carry):
            to = (g + d) % N_DP
            remote(pbuf.at[s, to], rv.at[s, g], ps_sem.at[s], pr_sem.at[s], (to, t)).start()
            return carry

        lax.fori_loop(1, N_DP, send_back, 0)

    def left(s):
        own = bt[s, :, bt_lanes]
        gram = lax.dot_general(
            own, bt[s], (((0,), (0,)), ((), ())), preferred_element_type=jnp.float32
        )
        ls[s] = decay_rate * ls[s] + (1.0 - decay_rate) * gram
        pltpu.make_async_copy(ls.at[s], nl_hbm.at[s], out_sem.at[2 + s]).start()

    gather_start(0)
    gather_start(1)
    gather_middle(0)
    for copy in later:
        copy.wait()
    gather_end(0)
    gather_middle(1)
    precondition(0)
    gather_end(1)
    precondition(1)
    left(0)
    left(1)

    for s in range(2):
        await_bytes(rv.at[s], pr_sem.at[s])

    def place(b, carry):
        slot = slot_of[b]
        up[b] = rv[slot % 2, slot // 2]
        return carry

    lax.fori_loop(0, NB, place, 0)
    write = pltpu.make_async_copy(up, up_hbm, out_sem.at[4])
    write.start()

    for k in range(4):
        for right in (True, False):
            az(k, right).wait_send()
            bz(k, right).wait_send()
    for k in range(2):
        for right in (True, False):
            by(k, right).wait_send()
            ay(k, right).wait_send()
            gxc(k, right).wait_send()
    gcc.wait_send()

    @pl.when(sends_g)
    def _():
        await_bytes(gsend.at[pl.ds(0, N_DP - 1), pl.ds(0, GX)], gs_sem)

    for s in range(2):
        await_bytes(sbuf.at[s, pl.ds(0, N_DP - 1)], ss_sem.at[s])
        for k in range(2):
            for right in (True, False):
                bxc(s, k, right).wait_send()
        for step in range(4):
            bcc(s, step).wait_send()
        await_bytes(norms.at[s, pl.ds(0, N_T - 1)], nsend_sem.at[s])
        await_bytes(pbuf.at[s, pl.ds(0, N_DP - 1)], ps_sem.at[s])
        pltpu.make_async_copy(rs.at[s], nr_hbm.at[s], out_sem.at[s]).wait()
        pltpu.make_async_copy(ls.at[s], nl_hbm.at[s], out_sem.at[2 + s]).wait()
    write.wait()


def body(
    layer_inputs,
    output_grads,
    left_stats,
    right_stats,
    left_roots,
    right_roots,
    owner_blocks,
    block_counts,
):
    f32, bf16 = jnp.float32, jnp.bfloat16
    live = jnp.arange(2, dtype=jnp.int32)[None, :] < block_counts[:, None]
    listed = jnp.where(live, jnp.clip(owner_blocks, 0, NB - 1), NB).reshape(-1)
    matches = listed[None, :] == jnp.arange(NB, dtype=jnp.int32)[:, None]
    slot_of = jnp.sum(
        jnp.where(matches, jnp.arange(2 * N_DP, dtype=jnp.int32)[None, :], 0), axis=1
    )
    dma = pltpu.SemaphoreType.DMA
    hbm = pl.BlockSpec(memory_space=pl.ANY)
    smem = pl.BlockSpec(memory_space=pltpu.SMEM)
    new_left, new_right, update = pl.pallas_call(
        kernel,
        out_shape=(
            jax.ShapeDtypeStruct((2, ROWS, BL), f32),
            jax.ShapeDtypeStruct((2, ROWS, BL), f32),
            jax.ShapeDtypeStruct((NB, 32, ROWS), bf16),
        ),
        in_specs=[hbm] * 6 + [smem] * 2,
        out_specs=(hbm, hbm, hbm),
        scratch_shapes=[
            pltpu.VMEM((NY, NZ, TOK, NRB * ROWS), bf16),
            pltpu.VMEM((TOK, SPAN * BL), bf16),
            pltpu.VMEM((N_DP, SPAN * CW, TOK), bf16),
            pltpu.VMEM((GROWS, N_DP * TOK), bf16),
            pltpu.VMEM((GROWS, NRB * ROWS), f32),
            pltpu.VMEM((NB + 1, CW, ROWS), bf16),
            pltpu.VMEM((2, N_DP, CW, ROWS), bf16),
            pltpu.VMEM((2, BL, BL), bf16),
            pltpu.VMEM((2, 2 * ROWS, BL), bf16),
            pltpu.VMEM((2, BL, BL), bf16),
            pltpu.VMEM((2, ROWS, BL), f32),
            pltpu.VMEM((2, ROWS, BL), f32),
            pltpu.VMEM((2, N_T, 16, ROWS), f32),
            pltpu.VMEM((2, N_DP, 32, ROWS), bf16),
            pltpu.VMEM((2, N_DP, 32, ROWS), bf16),
            pltpu.VMEM((NB, 32, ROWS), bf16),
            dma((6,)),
            dma((5,)),
            dma((45,)),
            dma((8,)),
            dma((4,)),
            dma((4,)),
            dma((8,)),
            dma,
            dma,
            dma((4,)),
            dma,
            dma((2,)),
            dma((2,)),
            dma((8,)),
            dma((8,)),
            dma((2,)),
            dma((2, N_T)),
            dma((2,)),
            dma((2,)),
        ],
        compiler_params=pltpu.CompilerParams(
            collective_id=0, has_side_effects=True, vmem_limit_bytes=48 * 1024 * 1024
        ),
        cost_estimate=pl.CostEstimate(
            flops=4_000_000_000, bytes_accessed=16_000_000, transcendentals=0
        ),
    )(
        layer_inputs.reshape(TOK, NRB * ROWS),
        output_grads,
        left_stats[0],
        right_stats[0],
        left_roots[0],
        right_roots[0],
        listed,
        slot_of,
    )
    update = update.reshape(NB, 4, BL).transpose(1, 0, 2).reshape(4, NRB, NCB * BL)
    return (new_left[None], new_right[None], update)


def solution(mesh):
    placed = (
        P("dp", None, "tensor"),
        P("dp", None),
        P("dp", None, "tensor", None),
        P("dp", None, "tensor", None),
        P("dp", None, "tensor", None),
        P("dp", None, None, None),
        P(),
        P(),
    )
    return jax.shard_map(
        body,
        mesh=mesh,
        in_specs=placed,
        out_specs=(
            P("dp", None, "tensor", None),
            P("dp", None, "tensor", None),
            P(("tensor", "dp"), None, None),
        ),
        check_vma=False,
    )
```

time: 404 us -> 118 us (0.29)
  waiting for transfers between devices: 288 us -> 0 us
  Pallas kernels: 0 us -> 108 us
  local copies, waits for them, and re-layouts: 36 us -> 7.82 us
  matrix products: 22.1 us -> 0 us
  other arithmetic: 18.2 us -> 0.8 us
  between operations: 14.1 us -> 0.67 us
  blocking collectives: 12 us -> 0 us
  starting transfers between devices: 9.91 us -> 0 us
    reduce_scatter x1 -> x0, waiting for transfers between devices: 244 us -> none  [body(): lax.psum_scatter(jnp.transpose(chosen, (1, 0, 2, 3)).reshape(tensor_rows...]
    pallas_call x0 -> x1, Pallas kernels: none -> 108 us  [body(): pl.pallas_call(kernel, out_shape=(jax.ShapeDtypeStruct((2, ROWS, BL), f32...]
    all_gather x1 -> x0, waiting for transfers between devices: 38.1 us -> none  [body(): full_blocks = lax.all_gather(summed, 'tensor', axis=0, tiled=True)]
    gather x2 -> x0, local copies, waits for them, and re-layouts: 32.7 us -> none  [body(): chosen = jnp.take(partials, listed, axis=1)]
    dot_general x5 -> x0, matrix products: 22.1 us -> none  [the longest x1 6.42 us: body(): jnp.einsum('tik,tc->kic', layer_inputs, output_grads, preferred_element_t...]
    convert_element_type x2 -> x0, other arithmetic: 16.1 us -> none  [the longest x1 15.9 us: body(): summed = lax.psum_scatter(jnp.transpose(chosen, (1, 0, 2, 3)).reshape(ten...]
    psum x1 -> x0, blocking collectives: 12 us -> none  [body(): grad_sq, prec_sq = lax.psum((grad_sq, prec_sq), 'tensor')]
    all_to_all x1 -> x0, starting transfers between devices: 9.83 us -> none  [body(): lax.all_to_all(grafted.reshape(groups, device_rows, slot_total, block_wid...]
  transfers between devices with their start and end apart: 3 -> 0, of which waited for: 3 -> 0; matrix products, arithmetic and copies ran while one was open for 2% -> 0% of each run, Pallas kernels for 0% -> 0%
where the time goes in v1:
time: 118 us
  Pallas kernels  108 us (92%)
  local copies, waits for them, and re-layouts  7.82 us (7%)
    pallas_call x1, Pallas kernels, body(): pl.pallas_call(kernel, out_shape=(jax.ShapeDtypeStruct((2, ROWS, BL), f32...  108 us
    unnamed x9, local copies, waits for them, and re-layouts  6.36 us

profile of v1, /device:TPU:1, one launch (start us, length us, event | category | flops | bytes accessed | tf_op | source)
XLA Modules:
  0.0 117.7 jit_solution(339689871981716304)
XLA Ops:
  0.6 0.7 compare_select_fusion
  1.3 0.1 copy.15
  1.4 0.1 reshape.21.send_idx
  1.5 0.1 select_reduce_fusion.slot_of
  1.6 0.9 copy.19
  2.6 0.0 copy-start
  2.6 1.2 %copy-done = f32[1,2,128,1024]{3,2,1,0:T(8,128)S(1)} copy-done((f32[1,2,128,1024]{3,2,1,0:T(8,128)S(1)}, f32[1,2,128,1024]{3,2,1,0:T(8,128)}, u32[]{:S(2)}) %copy-start) | copy-done | bytes 1048600
  3.8 0.0 copy-start.1
  3.8 1.2 %copy-done.1 = f32[1,2,128,1024]{3,2,1,0:T(8,128)S(1)} copy-done((f32[1,2,128,1024]{3,2,1,0:T(8,128)S(1)}, f32[1,2,128,1024]{3,2,1,0:T(8,128)}, u32[]{:S(2)}) %copy-start.1) | copy-done | bytes 1048600
  5.0 0.0 copy-start.2
  5.0 1.0 copy-done.2
  6.1 108.4 %shard_map.103 = (f32[2,128,1024]{2,1,0:T(8,128)S(1)}, f32[2,128,1024]{2,1,0:T(8,128)S(1)}, bf16[40,32,128]{2,1,0:T(8,128)(2,1)S(1)}) custom-call(bf16[128,512]{1,0:T(8,128)(2,1)S(1)} %bitcast.13, bf16[128,10240]{1,0:T(8,128)(2,1)} %g_hbm.1, f32[2,128,1024]{2,1,0:T(8,128)S(1)} %bitcast.14, f32[2,128,1024]{2,1,0:T(8,128)S(1)} %bitcast.15, ...), custom_call_target="tpu_custom_call" | custom-call | flops 4000000000 | bytes 16000000 | tf_op jit(solution)/shard_map/pallas_call | solution.py:470
  114.4 0.1 reshape.22
  114.5 0.1 copy.16
  114.6 1.1 reshape.23
  115.7 1.0 copy.22
  116.7 1.0 copy.23
Async XLA Ops:
  2.6 1.2 %copy-start = (f32[1,2,128,1024]{3,2,1,0:T(8,128)S(1)}, f32[1,2,128,1024]{3,2,1,0:T(8,128)}, u32[]{:S(2)}) copy-start(f32[1,2,128,1024]{3,2,1,0:T(8,128)} %param.10) | copy-start | bytes 3145732
  3.8 1.2 %copy-start.1 = (f32[1,2,128,1024]{3,2,1,0:T(8,128)S(1)}, f32[1,2,128,1024]{3,2,1,0:T(8,128)}, u32[]{:S(2)}) copy-start(f32[1,2,128,1024]{3,2,1,0:T(8,128)} %param.11) | copy-start | bytes 3145732
  5.0 1.0 copy-start.2

commit v2 on v1

v2 whole, which is shorter than its diff:
```python
import functools

import jax
import jax.numpy as jnp
from jax import lax
from jax.experimental import pallas as pl
from jax.experimental.pallas import tpu as pltpu
from jax.sharding import PartitionSpec as P

decay_rate = 0.99
epsilon = 1e-06

NY, NZ = 4, 8
NX = 4
N_DP = NY * NZ
N_T = NX * 2
BL = 1024
ROWS = 128
NRB, NCB = 4, 10
NB = NRB * NCB
TOK = 128
CW = BL // N_DP
GROWS = NCB * CW
GX = GROWS // NX
SPAN = 3
TA = 80
TAH = 48
TB = TOK - TA
TBH = 32
HALF = N_DP // 2

MESH = pl.DeviceIdType.MESH


def remote(src, dst, send_sem, recv_sem, device):
    return pltpu.make_async_remote_copy(
        src_ref=src,
        dst_ref=dst,
        send_sem=send_sem,
        recv_sem=recv_sem,
        device_id=device,
        device_id_type=MESH,
    )


def await_bytes(ref, sem):
    pltpu.make_async_copy(ref, ref, sem).wait()


def kernel(
    x_hbm,
    g_hbm,
    lr_hbm,
    rr_hbm,
    send_idx,
    slot_of,
    nl_out,
    nr_out,
    up_out,
    xall,
    gin,
    gsend,
    gt,
    acc,
    tiles,
    sbuf,
    bt,
    lhs,
    rr,
    pre,
    norms,
    pbuf,
    rv,
    load_sem,
    greet_sem,
    sent,
    az_sem,
    ay_sem,
    ay2_sem,
    by_sem,
    bz_sem,
    gs_sem,
    gr_sem,
    gx_sem,
    gc_sem,
    ss_sem,
    sr_sem,
    bx_sem,
    bc_sem,
    nsend_sem,
    nr_sem,
    ps_sem,
    pr_sem,
):
    g = lax.axis_index("dp")
    t = lax.axis_index("tensor")
    y, z = g // NZ, g % NZ
    x, core = t // 2, t % 2
    yp, ym = (y + 1) % NY, (y + NY - 1) % NY
    zp, zm = (z + 1) % NZ, (z + NZ - 1) % NZ
    xp, xm = (x + 1) % NX, (x + NX - 1) % NX
    dev_yp, dev_ym = (yp * NZ + z, t), (ym * NZ + z, t)
    dev_zp, dev_zm = (y * NZ + zp, t), (y * NZ + zm, t)
    dev_xp, dev_xm = (g, xp * 2 + core), (g, xm * 2 + core)
    dev_c = (g, x * 2 + 1 - core)
    lane_t = pl.multiple_of(t * ROWS, ROWS)
    both_ways = (True, False)

    barrier = pltpu.get_barrier_semaphore()
    z_line = [(y * NZ + (z + k) % NZ, t) for k in range(1, NZ)]
    y_line = [((y + k) % NY * NZ + z, t) for k in range(1, NY)]
    near = z_line + y_line + [dev_xp, dev_xm, dev_c]
    for device in near:
        pl.semaphore_signal(barrier, inc=1, device_id=device, device_id_type=MESH)

    j0 = (5 * x) // 2
    load_g = pltpu.make_async_copy(
        g_hbm.at[:, pl.ds(pl.multiple_of(j0 * BL, BL), SPAN * BL)], gin, load_sem.at[1]
    )
    load_g.start()
    own_x = pltpu.make_async_copy(x_hbm, xall.at[y, z], load_sem.at[0])
    own_x.start()
    later = [
        pltpu.make_async_copy(lr_hbm, lhs.at[:, pl.ds(ROWS, ROWS)], load_sem.at[2]),
        pltpu.make_async_copy(rr_hbm, rr, load_sem.at[3]),
    ]
    load_g.wait()
    sends_g = core == y // 2

    @pl.when(sends_g)
    def _():
        for j in range(SPAN):
            block = gin[:, j * BL : (j + 1) * BL].T
            gsend[:, j * CW : (j + 1) * CW, :] = block.reshape(N_DP, CW, TOK)

    own_x.wait()
    pl.semaphore_wait(barrier, len(near))

    z_off = (0, NZ - 1, 1, NZ - 2, 2, NZ - 3, 3, 4)

    def az(k, right):
        zs = (z + NZ - k) % NZ if right else (z + k) % NZ
        if k < 3:
            rows = pl.ds(0, TA)
        else:
            rows = pl.ds(0, TAH) if right else pl.ds(TAH, TA - TAH)
        ref = xall.at[y, zs, rows]
        n = k * 2 + (0 if right else 1)
        return remote(ref, ref, sent.at[n], az_sem.at[n], dev_zp if right else dev_zm)

    def ay(p, right):
        ref = xall.at[y, (z + z_off[p]) % NZ, pl.ds(0, TA)]
        n = p * 2 + (0 if right else 1)
        return remote(ref, ref, sent.at[8 + n], ay_sem.at[n], dev_yp if right else dev_ym)

    def ay2(p):
        right = p % 2 == 0
        ref = xall.at[ym if right else yp, (z + z_off[p]) % NZ, pl.ds(0, TA)]
        return remote(ref, ref, sent.at[24 + p], ay2_sem.at[p], dev_yp if right else dev_ym)

    def by(k, right):
        if k == 0:
            ys, rows = y, pl.ds(TA, TB)
        elif right:
            ys, rows = ym, pl.ds(TA, TBH)
        else:
            ys, rows = yp, pl.ds(TA + TBH, TB - TBH)
        ref = xall.at[ys, z, rows]
        n = k * 2 + (0 if right else 1)
        return remote(ref, ref, sent.at[32 + n], by_sem.at[n], dev_yp if right else dev_ym)

    def bz(q, k, right):
        ys = (y, ym, yp, (y + 2) % NY)[q]
        zs = (z + NZ - k) % NZ if right else (z + k) % NZ
        if k < 3:
            rows = pl.ds(TA, TB)
        else:
            rows = pl.ds(TA, TBH) if right else pl.ds(TA + TBH, TB - TBH)
        ref = xall.at[ys, zs, rows]
        n = q * 8 + k * 2 + (0 if right else 1)
        return remote(ref, ref, sent.at[36 + n], bz_sem.at[n], dev_zp if right else dev_zm)

    def az_step(k):
        for right in both_ways:
            az(k - 1, right).wait_recv()
            az(k, right).start()
            p = 2 * k - 1 if right else 2 * k
            for way in both_ways:
                ay(p, way).start()

    def bz_step(q, k):
        for right in both_ways:
            if k:
                bz(q, k - 1, right).wait_recv()
            bz(q, k, right).start()

    def ay2_step(p):
        ay(p, p % 2 == 0).wait_recv()
        ay2(p).start()

    for right in both_ways:
        az(0, right).start()
    for right in both_ways:
        by(0, right).start()

    for device in y_line:
        pl.semaphore_signal(greet_sem, inc=1, device_id=device, device_id_type=MESH)

    offset = pl.multiple_of(((5 * x) % 2) * 16, 16)
    gx_rows = pl.ds(pl.multiple_of(x * GX, 16), GX)
    own_lanes = pl.ds(pl.multiple_of(g * TOK, TOK), TOK)

    def send_g(to):
        remote(
            gsend.at[to, pl.ds(offset, GX)], gt.at[gx_rows, own_lanes], gs_sem, gr_sem, (to, t)
        ).start()

    @pl.when(sends_g)
    def _():
        pltpu.make_async_copy(
            gsend.at[g, pl.ds(offset, GX)], gt.at[gx_rows, own_lanes], gr_sem
        ).start()
        for k in range(1, NZ):
            send_g(y * NZ + (z + k) % NZ)

    for right in both_ways:
        ay(0, right).start()
    pl.semaphore_wait(greet_sem, len(y_line))

    @pl.when(sends_g)
    def _():
        def send_rest(d, carry):
            send_g((y * NZ + d) % N_DP)
            return carry

        lax.fori_loop(NZ, N_DP, send_rest, 0)

    half_lanes = pl.ds(pl.multiple_of(core * HALF * TOK, HALF * TOK), HALF * TOK)
    other_lanes = pl.ds(pl.multiple_of((1 - core) * HALF * TOK, HALF * TOK), HALF * TOK)

    quarter = HALF * TOK // 2

    def gxc(k, right):
        xs = x if k < 2 else (xm if right else xp)
        first = right if k != 1 else not right
        rows = pl.ds(pl.multiple_of(xs * GX, 16), GX)
        start = core * HALF * TOK + (0 if first else quarter)
        ref = gt.at[rows, pl.ds(pl.multiple_of(start, quarter), quarter)]
        n = k * 2 + (0 if right else 1)
        return remote(ref, ref, sent.at[68 + n], gx_sem.at[n], dev_xp if right else dev_xm)

    def gcc(step):
        rows = pl.ds(pl.multiple_of((x + NX - step) % NX * GX, 16), GX)
        ref = gt.at[rows, half_lanes]
        return remote(ref, ref, sent.at[74 + step], gc_sem.at[step], dev_c)

    def step_by():
        for right in both_ways:
            by(0, right).wait_recv()
        for right in both_ways:
            by(1, right).start()

    def step_by1():
        for right in both_ways:
            by(1, right).wait_recv()

    def step_G0():
        await_bytes(gt.at[gx_rows, half_lanes], gr_sem)
        for k in range(2):
            for right in both_ways:
                gxc(k, right).start()
        gcc(0).start()

    def step_G1():
        for right in both_ways:
            gxc(0, right).wait_recv()
            gxc(2, right).start()
        for right in both_ways:
            gxc(1, right).wait_recv()
            gcc(1 if right else 3).start()

    def step_G2():
        for right in both_ways:
            gxc(2, right).wait_recv()
        gcc(2).start()

    def step_ay7():
        for right in both_ways:
            az(3, right).wait_recv()
        for right in both_ways:
            ay(7, right).start()

    def step_L():
        for copy in later:
            copy.start()

    def step_GE():
        for step in (0, 1, 3, 2):
            gcc(step).wait_recv()

    def step_XE():
        for p in range(NZ):
            ay(p, p % 2 == 1).wait_recv()
        for q in range(NY):
            for right in both_ways:
                bz(q, 3, right).wait_recv()
        for p in range(NZ):
            ay2(p).wait_recv()

    bz_step(0, 0)
    az_step(1)
    step_by()
    bz_step(1, 0)
    bz_step(2, 0)
    bz_step(0, 1)
    az_step(2)
    ay2_step(0)
    step_G0()
    step_by1()
    bz_step(3, 0)
    bz_step(1, 1)
    bz_step(2, 1)
    step_L()
    bz_step(0, 2)
    step_G1()
    az_step(3)
    ay2_step(1)
    ay2_step(2)
    bz_step(3, 1)
    bz_step(1, 2)
    bz_step(2, 2)
    step_G2()
    bz_step(0, 3)
    step_ay7()
    ay2_step(3)
    ay2_step(4)
    bz_step(3, 2)
    bz_step(1, 3)
    bz_step(2, 3)
    ay2_step(5)
    ay2_step(6)
    bz_step(3, 3)
    ay2_step(7)
    step_XE()
    step_GE()

    acc[...] = jnp.zeros_like(acc)
    depth = 4 * TOK

    def add_tokens(n, carry):
        lanes = pl.ds(pl.multiple_of(n * depth, depth), depth)
        part = xall[n // 2, pl.ds((n % 2) * 4, 4)].reshape(depth, NRB * ROWS)
        acc[...] += jnp.dot(gt[:, lanes], part, preferred_element_type=jnp.float32)
        return carry

    lax.fori_loop(0, N_DP * TOK // depth, add_tokens, 0)
    for i in range(NRB):
        for j in range(NCB):
            tiles[i * NCB + j] = acc[
                j * CW : (j + 1) * CW, i * ROWS : (i + 1) * ROWS
            ].astype(jnp.bfloat16)
    tiles[NB] = jnp.zeros((CW, ROWS), jnp.bfloat16)

    bt_rows = pl.ds(pl.multiple_of(g * CW, CW), CW)
    bt_lanes = pl.ds(lane_t, ROWS)
    def send_blocks(s):
        def send_block(d, carry):
            to = (g + d) % N_DP
            sbuf[s, to] = tiles[send_idx[to * 2 + s]]
            remote(
                sbuf.at[s, to], bt.at[s, bt_rows, bt_lanes], ss_sem.at[s], sr_sem.at[s], (to, t)
            ).start()
            return carry

        sbuf[s, g] = tiles[send_idx[g * 2 + s]]
        pltpu.make_async_copy(sbuf.at[s, g], bt.at[s, bt_rows, bt_lanes], sr_sem.at[s]).start()
        lax.fori_loop(1, N_DP, send_block, 0)

    def lanes_of(xs, cs):
        return pl.ds(pl.multiple_of((xs * 2 + cs) * ROWS, ROWS), ROWS)

    def bxc(s, k, right):
        xs = x if k < 2 else (xm if right else xp)
        first = right if k != 1 else not right
        rows = pl.ds(0 if first else BL // 2, BL // 2)
        ref = bt.at[s, rows, lanes_of(xs, core)]
        n = s * 6 + k * 2 + (0 if right else 1)
        return remote(ref, ref, sent.at[78 + n], bx_sem.at[n], dev_xp if right else dev_xm)

    def bcc(s, step):
        ref = bt.at[s, :, lanes_of((x + NX - step) % NX, core)]
        n = s * 4 + step
        return remote(ref, ref, sent.at[90 + n], bc_sem.at[n], dev_c)

    def gather_start(s):
        await_bytes(bt.at[s, :, bt_lanes], sr_sem.at[s])
        for k in range(2):
            for right in both_ways:
                bxc(s, k, right).start()
        bcc(s, 0).start()

    def gather_middle(s):
        for right in both_ways:
            bxc(s, 0, right).wait_recv()
            bxc(s, 2, right).start()
        for right in both_ways:
            bxc(s, 1, right).wait_recv()
            bcc(s, 1 if right else 3).start()

    def gather_end(s):
        for right in both_ways:
            bxc(s, 2, right).wait_recv()
        bcc(s, 2).start()
        for step in (0, 1, 3, 2):
            bcc(s, step).wait_recv()

    def norm_copy(s, d):
        ref = norms.at[s, t]
        return remote(ref, ref, nsend_sem.at[s], nr_sem.at[s, d], (g, (t + d) % N_T))

    def precondition(s):
        lhs[s, 0:ROWS] = bt[s, pl.ds(lane_t, ROWS), :]
        both = lax.dot_general(
            lhs[s], bt[s], (((1,), (1,)), ((), ())), preferred_element_type=jnp.float32
        )
        nr_out[s] = both[0:ROWS]
        applied = both[ROWS:].astype(jnp.bfloat16)
        precond = jnp.dot(applied, rr[s], preferred_element_type=jnp.float32)
        pre[s] = precond
        own = bt[s, :, bt_lanes].astype(jnp.float32)
        norms[s, t, 0:8] = jnp.sum((own * own).reshape(-1, 8, ROWS), axis=0)
        squares = precond * precond
        folded = jnp.sum(squares.reshape(-1, 8, BL), axis=0)
        total = folded[:, 0:ROWS]
        for m in range(1, BL // ROWS):
            total = total + folded[:, m * ROWS : (m + 1) * ROWS]
        norms[s, t, 8:16] = total
        for d in range(1, N_T):
            norm_copy(s, d).start()

    def send_rows(s):
        for d in range(1, N_T):
            norm_copy(s, d).wait_recv()
        sums = jnp.sum(norms[s], axis=0)
        grad_sq = jnp.sum(sums[0:8], keepdims=True)
        prec_sq = jnp.sum(sums[8:16], keepdims=True)
        scale = jnp.sqrt(grad_sq) * lax.rsqrt(prec_sq + epsilon)
        grafted = pre[s] * scale
        pbuf[s] = grafted.reshape(ROWS, 8, ROWS).reshape(N_DP, 32, ROWS).astype(jnp.bfloat16)
        pltpu.make_async_copy(pbuf.at[s, g], rv.at[s, g], pr_sem.at[s]).start()

        def send_back(d, carry):
            to = (g + d) % N_DP
            remote(pbuf.at[s, to], rv.at[s, g], ps_sem.at[s], pr_sem.at[s], (to, t)).start()
            return carry

        lax.fori_loop(1, N_DP, send_back, 0)

    def left(s):
        own = bt[s, :, bt_lanes]
        nl_out[s] = lax.dot_general(
            own, bt[s], (((0,), (0,)), ((), ())), preferred_element_type=jnp.float32
        )

    send_blocks(0)
    gather_start(0)
    send_blocks(1)
    gather_middle(0)
    gather_start(1)
    for copy in later:
        copy.wait()
    gather_end(0)
    precondition(0)
    gather_middle(1)
    left(0)
    send_rows(0)
    gather_end(1)
    precondition(1)
    left(1)
    send_rows(1)

    for k in range(4):
        for right in both_ways:
            az(k, right).wait_send()
            for q in range(NY):
                bz(q, k, right).wait_send()
    for p in range(NZ):
        for right in both_ways:
            ay(p, right).wait_send()
        ay2(p).wait_send()
    for right in both_ways:
        for k in range(2):
            by(k, right).wait_send()
        for k in range(3):
            gxc(k, right).wait_send()
    for step in range(4):
        gcc(step).wait_send()

    @pl.when(sends_g)
    def _():
        await_bytes(gsend.at[pl.ds(0, N_DP - 1), pl.ds(0, GX)], gs_sem)

    for s in range(2):
        await_bytes(sbuf.at[s, pl.ds(0, N_DP - 1)], ss_sem.at[s])
        for k in range(3):
            for right in both_ways:
                bxc(s, k, right).wait_send()
        for step in range(4):
            bcc(s, step).wait_send()
        await_bytes(norms.at[s, pl.ds(0, N_T - 1)], nsend_sem.at[s])
        await_bytes(pbuf.at[s, pl.ds(0, N_DP - 1)], ps_sem.at[s])

    for s in range(2):
        await_bytes(rv.at[s], pr_sem.at[s])

    def place(b, carry):
        slot = slot_of[b]
        rows = rv[slot % 2, slot // 2]
        for k in range(4):
            up_out[k, b] = rows[k * 8 : (k + 1) * 8]
        return carry

    lax.fori_loop(0, NB, place, 0)

def body(
    layer_inputs,
    output_grads,
    left_stats,
    right_stats,
    left_roots,
    right_roots,
    owner_blocks,
    block_counts,
):
    f32, bf16 = jnp.float32, jnp.bfloat16
    live = jnp.arange(2, dtype=jnp.int32)[None, :] < block_counts[:, None]
    listed = jnp.where(live, jnp.clip(owner_blocks, 0, NB - 1), NB).reshape(-1)
    matches = listed[None, :] == jnp.arange(NB, dtype=jnp.int32)[:, None]
    slot_of = jnp.sum(
        jnp.where(matches, jnp.arange(2 * N_DP, dtype=jnp.int32)[None, :], 0), axis=1
    )
    dma = pltpu.SemaphoreType.DMA
    hbm = pl.BlockSpec(memory_space=pltpu.HBM)
    vmem = pl.BlockSpec(memory_space=pltpu.VMEM)
    smem = pl.BlockSpec(memory_space=pltpu.SMEM)
    left_gram, right_gram, update = pl.pallas_call(
        kernel,
        out_shape=(
            jax.ShapeDtypeStruct((2, ROWS, BL), f32),
            jax.ShapeDtypeStruct((2, ROWS, BL), f32),
            jax.ShapeDtypeStruct((4, NB, 8, ROWS), bf16),
        ),
        in_specs=[hbm] * 4 + [smem] * 2,
        out_specs=(vmem, vmem, vmem),
        scratch_shapes=[
            pltpu.VMEM((NY, NZ, TOK, NRB * ROWS), bf16),
            pltpu.VMEM((TOK, SPAN * BL), bf16),
            pltpu.VMEM((N_DP, SPAN * CW, TOK), bf16),
            pltpu.VMEM((GROWS, N_DP * TOK), bf16),
            pltpu.VMEM((GROWS, NRB * ROWS), f32),
            pltpu.VMEM((NB + 1, CW, ROWS), bf16),
            pltpu.VMEM((2, N_DP, CW, ROWS), bf16),
            pltpu.VMEM((2, BL, BL), bf16),
            pltpu.VMEM((2, 2 * ROWS, BL), bf16),
            pltpu.VMEM((2, BL, BL), bf16),
            pltpu.VMEM((2, ROWS, BL), f32),
            pltpu.VMEM((2, N_T, 16, ROWS), f32),
            pltpu.VMEM((2, N_DP, 32, ROWS), bf16),
            pltpu.VMEM((2, N_DP, 32, ROWS), bf16),
            dma((4,)),
            pltpu.SemaphoreType.REGULAR,
            dma((98,)),
            dma((8,)),
            dma((16,)),
            dma((8,)),
            dma((4,)),
            dma((32,)),
            dma,
            dma,
            dma((6,)),
            dma((4,)),
            dma((2,)),
            dma((2,)),
            dma((12,)),
            dma((8,)),
            dma((2,)),
            dma((2, N_T)),
            dma((2,)),
            dma((2,)),
        ],
        compiler_params=pltpu.CompilerParams(
            collective_id=0, has_side_effects=True, vmem_limit_bytes=48 * 1024 * 1024
        ),
        cost_estimate=pl.CostEstimate(
            flops=4_000_000_000, bytes_accessed=16_000_000, transcendentals=0
        ),
    )(
        layer_inputs.reshape(TOK, NRB * ROWS),
        output_grads,
        left_roots[0],
        right_roots[0],
        listed,
        slot_of,
    )
    update = update.reshape(4, NRB, NCB * BL)
    new_left = decay_rate * left_stats + (1.0 - decay_rate) * left_gram[None]
    new_right = decay_rate * right_stats + (1.0 - decay_rate) * right_gram[None]
    return (new_left, new_right, update)


def solution(mesh):
    placed = (
        P("dp", None, "tensor"),
        P("dp", None),
        P("dp", None, "tensor", None),
        P("dp", None, "tensor", None),
        P("dp", None, "tensor", None),
        P("dp", None, None, None),
        P(),
        P(),
    )
    return jax.shard_map(
        body,
        mesh=mesh,
        in_specs=placed,
        out_specs=(
            P("dp", None, "tensor", None),
            P("dp", None, "tensor", None),
            P(("tensor", "dp"), None, None),
        ),
        check_vma=False,
    )
```

time: 118 us -> 106 us (0.90)
  Pallas kernels: 108 us -> 98.2 us
  local copies, waits for them, and re-layouts: 7.82 us -> 4.72 us
  other arithmetic: 0.8 us -> 2.59 us
    pallas_call x1, Pallas kernels: 108 us -> 98.2 us  [body(): pl.pallas_call(kernel, out_shape=(jax.ShapeDtypeStruct((2, ROWS, BL), f32...]
    unnamed x9, local copies, waits for them, and re-layouts: 6.36 us -> 3.72 us
    add x0 -> x1, other arithmetic: none -> 1.79 us  [body(): new_right = decay_rate * right_stats + (1.0 - decay_rate) * right_gram[None]]
where the time goes in v2:
time: 106 us
  Pallas kernels  98.2 us (93%)
  local copies, waits for them, and re-layouts  4.72 us (4%)
  other arithmetic  2.59 us (2%)
    pallas_call x1, Pallas kernels, body(): pl.pallas_call(kernel, out_shape=(jax.ShapeDtypeStruct((2, ROWS, BL), f32...  98.2 us
    unnamed x9, local copies, waits for them, and re-layouts  3.72 us

profile of v2, /device:TPU:1, one launch (start us, length us, event | category | flops | bytes accessed | tf_op | source)
XLA Modules:
  0.0 106.2 jit_solution(14344398400357877478)
XLA Ops:
  0.6 0.7 compare_select_fusion
  1.3 0.1 copy.13
  1.4 0.1 reshape.20.send_idx
  1.5 0.1 select_reduce_fusion.slot_of
  1.6 0.9 copy.16
  2.6 0.0 copy-start
  2.6 1.7 %copy-done = bf16[128,10240]{1,0:T(8,128)(2,1)S(1)} copy-done((bf16[128,10240]{1,0:T(8,128)(2,1)S(1)}, bf16[128,10240]{1,0:T(8,128)(2,1)}, u32[]{:S(2)}) %copy-start) | copy-done | bytes 2621464
  4.3 0.0 copy-start.1
  4.3 1.0 copy-done.1
  5.3 0.0 copy-start.2
  5.4 0.0 copy-start.3
  5.4 98.2 %shard_map.103 = (f32[2,128,1024]{2,1,0:T(8,128)S(1)}, f32[2,128,1024]{2,1,0:T(8,128)S(1)}, bf16[4,40,8,128]{3,2,1,0:T(8,128)(2,1)S(1)}) custom-call(bf16[128,512]{1,0:T(8,128)(2,1)S(1)} %bitcast.12, bf16[128,10240]{1,0:T(8,128)(2,1)S(1)} %copy-done, bf16[2,128,1024]{2,1,0:T(8,128)(2,1)S(1)} %bitcast.13, bf16[2,1024,1024]{2,1,0:T(8,128)(2,1)} %bitcast.15, ...), custom_call_target="tpu_custom_call" | custom-call | flops 4000000000 | bytes 16000000 | tf_op jit(solution)/shard_map/pallas_call | solution.py:546
  103.6 0.0 copy-done.2
  103.6 0.0 copy-done.3
  103.6 1.8 %bitcast_add_fusion = (f32[1,2,128,1024]{3,2,1,0:T(8,128)}, f32[1,2,128,1024]{3,2,1,0:T(8,128)}) fusion(f32[2,128,1024]{2,1,0:T(8,128)S(1)} %get-tuple-element.7, f32[1,2,128,1024]{3,2,1,0:T(8,128)S(1)} %copy-done.2, f32[2,128,1024]{2,1,0:T(8,128)S(1)} %get-tuple-element.6, f32[1,2,128,1024]{3,2,1,0:T(8,128)S(1)} %copy-done.3), kind=kLoop, calls=%fused_computation | loop fusion | flops 1572864 | bytes 6291456 | tf_op jit(solution)/shard_map/add | solution.py:607
  105.4 0.8 reshape.21
Async XLA Ops:
  2.6 1.7 %copy-start = (bf16[128,10240]{1,0:T(8,128)(2,1)S(1)}, bf16[128,10240]{1,0:T(8,128)(2,1)}, u32[]{:S(2)}) copy-start(bf16[128,10240]{1,0:T(8,128)(2,1)} %g_hbm.1) | copy-start | bytes 7864324
  4.3 1.0 copy-start.1
  5.3 98.2 %copy-start.2 = (f32[1,2,128,1024]{3,2,1,0:T(8,128)S(1)}, f32[1,2,128,1024]{3,2,1,0:T(8,128)}, u32[]{:S(2)}) copy-start(f32[1,2,128,1024]{3,2,1,0:T(8,128)} %param.11) | copy-start | bytes 3145732
  5.4 98.2 %copy-start.3 = (f32[1,2,128,1024]{3,2,1,0:T(8,128)S(1)}, f32[1,2,128,1024]{3,2,1,0:T(8,128)}, u32[]{:S(2)}) copy-start(f32[1,2,128,1024]{3,2,1,0:T(8,128)} %param.10) | copy-start | bytes 3145732

commit v3 on v2

--- a/solution.py
+++ b/solution.py
@@ -52,8 +52,8 @@
     g_hbm,
     lr_hbm,
     rr_hbm,
-    send_idx,
-    slot_of,
+    listed,
+    counts,
     nl_out,
     nr_out,
     up_out,
@@ -71,6 +71,7 @@
     norms,
     pbuf,
     rv,
+    slot_of,
     load_sem,
     greet_sem,
     sent,
@@ -227,13 +228,11 @@
         ay(0, right).start()
     pl.semaphore_wait(greet_sem, len(y_line))
 
-    @pl.when(sends_g)
-    def _():
-        def send_rest(d, carry):
-            send_g((y * NZ + d) % N_DP)
-            return carry
-
-        lax.fori_loop(NZ, N_DP, send_rest, 0)
+    def send_g_row(k):
+        @pl.when(sends_g)
+        def _():
+            for n in range(NZ):
+                send_g((y + k) % NY * NZ + (z + n) % NZ)
 
     half_lanes = pl.ds(pl.multiple_of(core * HALF * TOK, HALF * TOK), HALF * TOK)
     other_lanes = pl.ds(pl.multiple_of((1 - core) * HALF * TOK, HALF * TOK), HALF * TOK)
@@ -294,66 +293,66 @@
         for copy in later:
             copy.start()
 
-    def step_GE():
-        for step in (0, 1, 3, 2):
-            gcc(step).wait_recv()
-
-    def step_XE():
-        for p in range(NZ):
-            ay(p, p % 2 == 1).wait_recv()
-        for q in range(NY):
-            for right in both_ways:
-                bz(q, 3, right).wait_recv()
-        for p in range(NZ):
-            ay2(p).wait_recv()
-
+    az_step(1)
+    send_g_row(1)
+    step_by()
+    send_g_row(2)
+    az_step(2)
+    send_g_row(3)
     bz_step(0, 0)
-    az_step(1)
-    step_by()
+    ay2_step(0)
     bz_step(1, 0)
     bz_step(2, 0)
+    az_step(3)
+    step_L()
+    ay2_step(1)
+    ay2_step(2)
     bz_step(0, 1)
-    az_step(2)
-    ay2_step(0)
-    step_G0()
     step_by1()
     bz_step(3, 0)
+    step_G0()
     bz_step(1, 1)
     bz_step(2, 1)
-    step_L()
-    bz_step(0, 2)
-    step_G1()
-    az_step(3)
-    ay2_step(1)
-    ay2_step(2)
-    bz_step(3, 1)
-    bz_step(1, 2)
-    bz_step(2, 2)
-    step_G2()
-    bz_step(0, 3)
     step_ay7()
     ay2_step(3)
     ay2_step(4)
+    bz_step(0, 2)
+    bz_step(3, 1)
+    ay2_step(5)
+    ay2_step(6)
+    bz_step(1, 2)
+    bz_step(2, 2)
+    step_G1()
+    bz_step(0, 3)
     bz_step(3, 2)
+    ay2_step(7)
     bz_step(1, 3)
     bz_step(2, 3)
-    ay2_step(5)
-    ay2_step(6)
     bz_step(3, 3)
-    ay2_step(7)
-    step_XE()
-    step_GE()
-
-    acc[...] = jnp.zeros_like(acc)
-    depth = 4 * TOK
-
-    def add_tokens(n, carry):
-        lanes = pl.ds(pl.multiple_of(n * depth, depth), depth)
-        part = xall[n // 2, pl.ds((n % 2) * 4, 4)].reshape(depth, NRB * ROWS)
-        acc[...] += jnp.dot(gt[:, lanes], part, preferred_element_type=jnp.float32)
-        return carry
-
-    lax.fori_loop(0, N_DP * TOK // depth, add_tokens, 0)
+    step_G2()
+
+    def add_tokens(ys):
+        lanes = pl.ds(pl.multiple_of(ys * NZ * TOK, NZ * TOK), NZ * TOK)
+        part = xall[ys].reshape(NZ * TOK, NRB * ROWS)
+        return jnp.dot(gt[:, lanes], part, preferred_element_type=jnp.float32)
+
+    for step in (0, 1, 3, 2):
+        gcc(step).wait_recv()
+    for right in both_ways:
+        bz(0, 3, right).wait_recv()
+    acc[...] = add_tokens(y)
+    for p in range(NZ):
+        ay(p, p % 2 == 1).wait_recv()
+    for q in (1, 2):
+        for right in both_ways:
+            bz(q, 3, right).wait_recv()
+    acc[...] += add_tokens(ym)
+    acc[...] += add_tokens(yp)
+    for p in range(NZ):
+        ay2(p).wait_recv()
+    for right in both_ways:
+        bz(3, 3, right).wait_recv()
+    acc[...] += add_tokens((y + 2) % NY)
     for i in range(NRB):
         for j in range(NCB):
             tiles[i * NCB + j] = acc[
@@ -363,16 +362,20 @@
 
     bt_rows = pl.ds(pl.multiple_of(g * CW, CW), CW)
     bt_lanes = pl.ds(lane_t, ROWS)
+    def listed_block(to, s):
+        block = jnp.clip(listed[to * 2 + s], 0, NB - 1)
+        return jnp.where(s < counts[to], block, NB)
+
     def send_blocks(s):
         def send_block(d, carry):
             to = (g + d) % N_DP
-            sbuf[s, to] = tiles[send_idx[to * 2 + s]]
+            sbuf[s, to] = tiles[listed_block(to, s)]
             remote(
                 sbuf.at[s, to], bt.at[s, bt_rows, bt_lanes], ss_sem.at[s], sr_sem.at[s], (to, t)
             ).start()
             return carry
 
-        sbuf[s, g] = tiles[send_idx[g * 2 + s]]
+        sbuf[s, g] = tiles[listed_block(g, s)]
         pltpu.make_async_copy(sbuf.at[s, g], bt.at[s, bt_rows, bt_lanes], sr_sem.at[s]).start()
         lax.fori_loop(1, N_DP, send_block, 0)
 
@@ -398,6 +401,8 @@
             for right in both_ways:
                 bxc(s, k, right).start()
         bcc(s, 0).start()
+        own = bt[s, :, bt_lanes].astype(jnp.float32)
+        norms[s, t, 0:8] = jnp.sum((own * own).reshape(-1, 8, ROWS), axis=0)
 
     def gather_middle(s):
         for right in both_ways:
@@ -427,8 +432,6 @@
         applied = both[ROWS:].astype(jnp.bfloat16)
         precond = jnp.dot(applied, rr[s], preferred_element_type=jnp.float32)
         pre[s] = precond
-        own = bt[s, :, bt_lanes].astype(jnp.float32)
-        norms[s, t, 0:8] = jnp.sum((own * own).reshape(-1, 8, ROWS), axis=0)
         squares = precond * precond
         folded = jnp.sum(squares.reshape(-1, 8, BL), axis=0)
         total = folded[:, 0:ROWS]
@@ -510,6 +513,13 @@
         await_bytes(norms.at[s, pl.ds(0, N_T - 1)], nsend_sem.at[s])
         await_bytes(pbuf.at[s, pl.ds(0, N_DP - 1)], ps_sem.at[s])
 
+    lane = lax.broadcasted_iota(jnp.int32, (8, ROWS), 1)
+    slots = jnp.zeros((8, ROWS), jnp.int32)
+    for slot in range(2 * N_DP):
+        slots = jnp.where(lane == listed_block(slot // 2, slot % 2), slot, slots)
+    for b in range(NB):
+        slot_of[b] = jnp.max(jnp.where(lane == b, slots, 0))
+
     for s in range(2):
         await_bytes(rv.at[s], pr_sem.at[s])
 
@@ -533,12 +543,6 @@
     block_counts,
 ):
     f32, bf16 = jnp.float32, jnp.bfloat16
-    live = jnp.arange(2, dtype=jnp.int32)[None, :] < block_counts[:, None]
-    listed = jnp.where(live, jnp.clip(owner_blocks, 0, NB - 1), NB).reshape(-1)
-    matches = listed[None, :] == jnp.arange(NB, dtype=jnp.int32)[:, None]
-    slot_of = jnp.sum(
-        jnp.where(matches, jnp.arange(2 * N_DP, dtype=jnp.int32)[None, :], 0), axis=1
-    )
     dma = pltpu.SemaphoreType.DMA
     hbm = pl.BlockSpec(memory_space=pltpu.HBM)
     vmem = pl.BlockSpec(memory_space=pltpu.VMEM)
@@ -567,6 +571,7 @@
             pltpu.VMEM((2, N_T, 16, ROWS), f32),
             pltpu.VMEM((2, N_DP, 32, ROWS), bf16),
             pltpu.VMEM((2, N_DP, 32, ROWS), bf16),
+            pltpu.SMEM((NB,), jnp.int32),
             dma((4,)),
             pltpu.SemaphoreType.REGULAR,
             dma((98,)),
@@ -599,8 +604,8 @@
         output_grads,
         left_roots[0],
         right_roots[0],
-        listed,
-        slot_of,
+        owner_blocks.reshape(-1),
+        block_counts,
     )
     update = update.reshape(4, NRB, NCB * BL)
     new_left = decay_rate * left_stats + (1.0 - decay_rate) * left_gram[None]

time: 106 us -> 98.3 us (0.927)
  Pallas kernels: 98.2 us -> 89.6 us
  local copies, waits for them, and re-layouts: 4.72 us -> 6.03 us
    pallas_call x1, Pallas kernels: 98.2 us -> 89.6 us  [body(): pl.pallas_call(kernel, out_shape=(jax.ShapeDtypeStruct((2, ROWS, BL), f32...]
    unnamed x9 -> x12, local copies, waits for them, and re-layouts: 3.72 us -> 5.13 us
where the time goes in v3:
time: 98.3 us; the launch traced here: 98.1 us
  Pallas kernels  89.6 us (91%)
  local copies, waits for them, and re-layouts  6.03 us (6%)
  other arithmetic  1.79 us (2%)
    pallas_call x1, Pallas kernels, body(): pl.pallas_call(kernel, out_shape=(jax.ShapeDtypeStruct((2, ROWS, BL), f32...  89.6 us
    unnamed x12, local copies, waits for them, and re-layouts  5.13 us

profile of v3, /device:TPU:1, one launch (start us, length us, event | category | flops | bytes accessed | tf_op | source)
XLA Modules:
  0.0 98.1 jit_solution(11387046201160339542)
XLA Ops:
  0.6 0.8 copy.12
  1.4 0.1 reshape.18.listed
  1.5 0.9 copy.15
  2.4 0.0 copy-start
  2.4 1.7 %copy-done = bf16[128,10240]{1,0:T(8,128)(2,1)S(1)} copy-done((bf16[128,10240]{1,0:T(8,128)(2,1)S(1)}, bf16[128,10240]{1,0:T(8,128)(2,1)}, u32[]{:S(2)}) %copy-start) | copy-done | bytes 2621464
  4.2 0.0 copy-start.1
  4.2 1.0 %copy-done.1 = bf16[1,2,128,1024]{3,2,1,0:T(8,128)(2,1)S(1)} copy-done((bf16[1,2,128,1024]{3,2,1,0:T(8,128)(2,1)S(1)}, bf16[1,2,128,1024]{3,2,1,0:T(8,128)(2,1)}, u32[]{:S(2)}) %copy-start.1) | copy-done | bytes 524312
  5.2 0.0 copy-start.2
  5.2 0.7 copy-done.2
  5.9 0.0 copy-start.3
  5.9 0.0 copy-start.4
  5.9 89.6 %shard_map.103 = (f32[2,128,1024]{2,1,0:T(8,128)S(1)}, f32[2,128,1024]{2,1,0:T(8,128)S(1)}, bf16[4,40,8,128]{3,2,1,0:T(8,128)(2,1)S(1)}) custom-call(bf16[128,512]{1,0:T(8,128)(2,1)S(1)} %bitcast.12, bf16[128,10240]{1,0:T(8,128)(2,1)S(1)} %copy-done, bf16[2,128,1024]{2,1,0:T(8,128)(2,1)S(1)} %bitcast.13, bf16[2,1024,1024]{2,1,0:T(8,128)(2,1)} %bitcast.15, ...), custom_call_target="tpu_custom_call" | custom-call | flops 4000000000 | bytes 16000000 | tf_op jit(solution)/shard_map/pallas_call | solution.py:550
  95.5 0.0 copy-done.3
  95.5 0.0 copy-done.4
  95.5 1.8 %bitcast_add_fusion = (f32[1,2,128,1024]{3,2,1,0:T(8,128)}, f32[1,2,128,1024]{3,2,1,0:T(8,128)}) fusion(f32[2,128,1024]{2,1,0:T(8,128)S(1)} %get-tuple-element.7, f32[1,2,128,1024]{3,2,1,0:T(8,128)S(1)} %copy-done.3, f32[2,128,1024]{2,1,0:T(8,128)S(1)} %get-tuple-element.6, f32[1,2,128,1024]{3,2,1,0:T(8,128)S(1)} %copy-done.4), kind=kLoop, calls=%fused_computation | loop fusion | flops 1572864 | bytes 6291456 | tf_op jit(solution)/shard_map/add | solution.py:612
  97.3 0.8 reshape.19
Async XLA Ops:
  2.4 1.7 %copy-start = (bf16[128,10240]{1,0:T(8,128)(2,1)S(1)}, bf16[128,10240]{1,0:T(8,128)(2,1)}, u32[]{:S(2)}) copy-start(bf16[128,10240]{1,0:T(8,128)(2,1)} %g_hbm.1) | copy-start | bytes 7864324
  4.2 1.0 %copy-start.1 = (bf16[1,2,128,1024]{3,2,1,0:T(8,128)(2,1)S(1)}, bf16[1,2,128,1024]{3,2,1,0:T(8,128)(2,1)}, u32[]{:S(2)}) copy-start(bf16[1,2,128,1024]{3,2,1,0:T(8,128)(2,1)} %param.12) | copy-start | bytes 1572868
  5.2 0.7 copy-start.2
  5.9 89.6 %copy-start.3 = (f32[1,2,128,1024]{3,2,1,0:T(8,128)S(1)}, f32[1,2,128,1024]{3,2,1,0:T(8,128)}, u32[]{:S(2)}) copy-start(f32[1,2,128,1024]{3,2,1,0:T(8,128)} %param.11) | copy-start | bytes 3145732
  5.9 89.7 %copy-start.4 = (f32[1,2,128,1024]{3,2,1,0:T(8,128)S(1)}, f32[1,2,128,1024]{3,2,1,0:T(8,128)}, u32[]{:S(2)}) copy-start(f32[1,2,128,1024]{3,2,1,0:T(8,128)} %param.10) | copy-start | bytes 3145732

commit v4 on v3

--- a/solution.py
+++ b/solution.py
@@ -53,7 +53,6 @@
     lr_hbm,
     rr_hbm,
     listed,
-    counts,
     nl_out,
     nr_out,
     up_out,
@@ -363,21 +362,20 @@
     bt_rows = pl.ds(pl.multiple_of(g * CW, CW), CW)
     bt_lanes = pl.ds(lane_t, ROWS)
     def listed_block(to, s):
-        block = jnp.clip(listed[to * 2 + s], 0, NB - 1)
-        return jnp.where(s < counts[to], block, NB)
+        return listed[s, to]
 
     def send_blocks(s):
-        def send_block(d, carry):
+        def send_block(d):
             to = (g + d) % N_DP
             sbuf[s, to] = tiles[listed_block(to, s)]
             remote(
                 sbuf.at[s, to], bt.at[s, bt_rows, bt_lanes], ss_sem.at[s], sr_sem.at[s], (to, t)
             ).start()
-            return carry
 
         sbuf[s, g] = tiles[listed_block(g, s)]
         pltpu.make_async_copy(sbuf.at[s, g], bt.at[s, bt_rows, bt_lanes], sr_sem.at[s]).start()
-        lax.fori_loop(1, N_DP, send_block, 0)
+        for d in range(1, N_DP):
+            send_block(d)
 
     def lanes_of(xs, cs):
         return pl.ds(pl.multiple_of((xs * 2 + cs) * ROWS, ROWS), ROWS)
@@ -516,21 +514,18 @@
     lane = lax.broadcasted_iota(jnp.int32, (8, ROWS), 1)
     slots = jnp.zeros((8, ROWS), jnp.int32)
     for slot in range(2 * N_DP):
-        slots = jnp.where(lane == listed_block(slot // 2, slot % 2), slot, slots)
+        slots = jnp.where(lane == listed_block(slot % N_DP, slot // N_DP), slot, slots)
     for b in range(NB):
         slot_of[b] = jnp.max(jnp.where(lane == b, slots, 0))
 
     for s in range(2):
         await_bytes(rv.at[s], pr_sem.at[s])
 
-    def place(b, carry):
+    for b in range(NB):
         slot = slot_of[b]
-        rows = rv[slot % 2, slot // 2]
+        rows = rv[slot // N_DP, slot % N_DP]
         for k in range(4):
             up_out[k, b] = rows[k * 8 : (k + 1) * 8]
-        return carry
-
-    lax.fori_loop(0, NB, place, 0)
 
 def body(
     layer_inputs,
@@ -543,6 +538,8 @@
     block_counts,
 ):
     f32, bf16 = jnp.float32, jnp.bfloat16
+    live = jnp.arange(2, dtype=jnp.int32)[:, None] < block_counts[None, :]
+    listed = jnp.where(live, jnp.clip(owner_blocks.T, 0, NB - 1), NB)
     dma = pltpu.SemaphoreType.DMA
     hbm = pl.BlockSpec(memory_space=pltpu.HBM)
     vmem = pl.BlockSpec(memory_space=pltpu.VMEM)
@@ -554,7 +551,7 @@
             jax.ShapeDtypeStruct((2, ROWS, BL), f32),
             jax.ShapeDtypeStruct((4, NB, 8, ROWS), bf16),
         ),
-        in_specs=[hbm] * 4 + [smem] * 2,
+        in_specs=[hbm] * 4 + [smem],
         out_specs=(vmem, vmem, vmem),
         scratch_shapes=[
             pltpu.VMEM((NY, NZ, TOK, NRB * ROWS), bf16),
@@ -594,7 +591,7 @@
             dma((2,)),
         ],
         compiler_params=pltpu.CompilerParams(
-            collective_id=0, has_side_effects=True, vmem_limit_bytes=48 * 1024 * 1024
+            collective_id=0, has_side_effects=True, vmem_limit_bytes=50 * 1024 * 1024
         ),
         cost_estimate=pl.CostEstimate(
             flops=4_000_000_000, bytes_accessed=16_000_000, transcendentals=0
@@ -604,8 +601,7 @@
         output_grads,
         left_roots[0],
         right_roots[0],
-        owner_blocks.reshape(-1),
-        block_counts,
+        listed,
     )
     update = update.reshape(4, NRB, NCB * BL)
     new_left = decay_rate * left_stats + (1.0 - decay_rate) * left_gram[None]

time: 98.3 us -> 95.8 us (0.975)
  local copies, waits for them, and re-layouts: 6.03 us -> 2.77 us
    unnamed x12 -> x7, local copies, waits for them, and re-layouts: 5.13 us -> 1.97 us
where the time goes in v4:
time: 95.8 us; the launch traced here: 95.5 us
  Pallas kernels  89.6 us (94%)
  local copies, waits for them, and re-layouts  2.77 us (3%)
  other arithmetic  2.48 us (3%)
    pallas_call x1, Pallas kernels, body(): pl.pallas_call(kernel, out_shape=(jax.ShapeDtypeStruct((2, ROWS, BL), f32...  89.6 us
    unnamed x7, local copies, waits for them, and re-layouts  1.97 us

profile of v4, /device:TPU:1, one launch (start us, length us, event | category | flops | bytes accessed | tf_op | source)
XLA Modules:
  0.0 95.5 jit_solution(1856157770580275221)
XLA Ops:
  0.6 0.7 compare_select_fusion.listed
  1.3 0.9 copy.13
  2.2 0.0 copy-start
  2.3 1.0 %copy-done = bf16[1,2,128,1024]{3,2,1,0:T(8,128)(2,1)S(1)} copy-done((bf16[1,2,128,1024]{3,2,1,0:T(8,128)(2,1)S(1)}, bf16[1,2,128,1024]{3,2,1,0:T(8,128)(2,1)}, u32[]{:S(2)}) %copy-start) | copy-done | bytes 524312
  3.3 0.0 copy-start.1
  3.3 0.0 copy-start.2
  3.3 89.6 %shard_map.103 = (f32[2,128,1024]{2,1,0:T(8,128)S(1)}, f32[2,128,1024]{2,1,0:T(8,128)S(1)}, bf16[4,40,8,128]{3,2,1,0:T(8,128)(2,1)S(1)}) custom-call(bf16[128,512]{1,0:T(8,128)(2,1)S(1)} %bitcast.14, bf16[128,10240]{1,0:T(8,128)(2,1)} %g_hbm.1, bf16[2,128,1024]{2,1,0:T(8,128)(2,1)S(1)} %bitcast.15, bf16[2,1024,1024]{2,1,0:T(8,128)(2,1)} %bitcast.17, ...), custom_call_target="tpu_custom_call" | custom-call | flops 4000000000 | bytes 16000000 | tf_op jit(solution)/shard_map/pallas_call | solution.py:547
  92.9 0.0 copy-done.1
  92.9 0.0 copy-done.2
  92.9 1.8 %bitcast_add_fusion = (f32[1,2,128,1024]{3,2,1,0:T(8,128)}, f32[1,2,128,1024]{3,2,1,0:T(8,128)}) fusion(f32[2,128,1024]{2,1,0:T(8,128)S(1)} %get-tuple-element.7, f32[1,2,128,1024]{3,2,1,0:T(8,128)S(1)} %copy-done.1, f32[2,128,1024]{2,1,0:T(8,128)S(1)} %get-tuple-element.6, f32[1,2,128,1024]{3,2,1,0:T(8,128)S(1)} %copy-done.2), kind=kLoop, calls=%fused_computation | loop fusion | flops 1572864 | bytes 6291456 | tf_op jit(solution)/shard_map/add | solution.py:608
  94.7 0.8 reshape.16
Async XLA Ops:
  2.2 1.0 %copy-start = (bf16[1,2,128,1024]{3,2,1,0:T(8,128)(2,1)S(1)}, bf16[1,2,128,1024]{3,2,1,0:T(8,128)(2,1)}, u32[]{:S(2)}) copy-start(bf16[1,2,128,1024]{3,2,1,0:T(8,128)(2,1)} %param.12) | copy-start | bytes 1572868
  3.3 89.6 %copy-start.1 = (f32[1,2,128,1024]{3,2,1,0:T(8,128)S(1)}, f32[1,2,128,1024]{3,2,1,0:T(8,128)}, u32[]{:S(2)}) copy-start(f32[1,2,128,1024]{3,2,1,0:T(8,128)} %param.11) | copy-start | bytes 3145732
  3.3 89.6 %copy-start.2 = (f32[1,2,128,1024]{3,2,1,0:T(8,128)S(1)}, f32[1,2,128,1024]{3,2,1,0:T(8,128)}, u32[]{:S(2)}) copy-start(f32[1,2,128,1024]{3,2,1,0:T(8,128)} %param.10) | copy-start | bytes 3145732

commit v5 on v4

--- a/solution.py
+++ b/solution.py
@@ -426,10 +426,8 @@
         both = lax.dot_general(
             lhs[s], bt[s], (((1,), (1,)), ((), ())), preferred_element_type=jnp.float32
         )
-        nr_out[s] = both[0:ROWS]
         applied = both[ROWS:].astype(jnp.bfloat16)
         precond = jnp.dot(applied, rr[s], preferred_element_type=jnp.float32)
-        pre[s] = precond
         squares = precond * precond
         folded = jnp.sum(squares.reshape(-1, 8, BL), axis=0)
         total = folded[:, 0:ROWS]
@@ -438,6 +436,8 @@
         norms[s, t, 8:16] = total
         for d in range(1, N_T):
             norm_copy(s, d).start()
+        pre[s] = precond.reshape(ROWS, 8, ROWS).reshape(8 * ROWS, ROWS)
+        nr_out[s] = both[0:ROWS]
 
     def send_rows(s):
         for d in range(1, N_T):
@@ -446,8 +446,7 @@
         grad_sq = jnp.sum(sums[0:8], keepdims=True)
         prec_sq = jnp.sum(sums[8:16], keepdims=True)
         scale = jnp.sqrt(grad_sq) * lax.rsqrt(prec_sq + epsilon)
-        grafted = pre[s] * scale
-        pbuf[s] = grafted.reshape(ROWS, 8, ROWS).reshape(N_DP, 32, ROWS).astype(jnp.bfloat16)
+        pbuf[s] = (pre[s] * scale).reshape(N_DP, 32, ROWS).astype(jnp.bfloat16)
         pltpu.make_async_copy(pbuf.at[s, g], rv.at[s, g], pr_sem.at[s]).start()
 
         def send_back(d, carry):
@@ -473,10 +472,10 @@
     gather_end(0)
     precondition(0)
     gather_middle(1)
-    left(0)
     send_rows(0)
     gather_end(1)
     precondition(1)
+    left(0)
     left(1)
     send_rows(1)
 
@@ -564,7 +563,7 @@
             pltpu.VMEM((2, BL, BL), bf16),
             pltpu.VMEM((2, 2 * ROWS, BL), bf16),
             pltpu.VMEM((2, BL, BL), bf16),
-            pltpu.VMEM((2, ROWS, BL), f32),
+            pltpu.VMEM((2, 8 * ROWS, ROWS), f32),
             pltpu.VMEM((2, N_T, 16, ROWS), f32),
             pltpu.VMEM((2, N_DP, 32, ROWS), bf16),
             pltpu.VMEM((2, N_DP, 32, ROWS), bf16),

time: 95.8 us -> 95.9 us (level)
  no operation moved by 1% of the time
where the time goes in v5:
time: 95.9 us; the launch traced here: 95.7 us
  Pallas kernels  89.8 us (94%)
  local copies, waits for them, and re-layouts  2.77 us (3%)
  other arithmetic  2.48 us (3%)
    pallas_call x1, Pallas kernels, body(): pl.pallas_call(kernel, out_shape=(jax.ShapeDtypeStruct((2, ROWS, BL), f32...  89.8 us
    unnamed x7, local copies, waits for them, and re-layouts  1.97 us

profile of v5, /device:TPU:1, one launch (start us, length us, event | category | flops | bytes accessed | tf_op | source)
XLA Modules:
  0.0 95.7 jit_solution(17139776331676094206)
XLA Ops:
  0.6 0.7 compare_select_fusion.listed
  1.3 0.9 copy.13
  2.2 0.0 copy-start
  2.3 1.0 %copy-done = bf16[1,2,128,1024]{3,2,1,0:T(8,128)(2,1)S(1)} copy-done((bf16[1,2,128,1024]{3,2,1,0:T(8,128)(2,1)S(1)}, bf16[1,2,128,1024]{3,2,1,0:T(8,128)(2,1)}, u32[]{:S(2)}) %copy-start) | copy-done | bytes 524312
  3.3 0.0 copy-start.1
  3.3 0.0 copy-start.2
  3.3 89.8 %shard_map.103 = (f32[2,128,1024]{2,1,0:T(8,128)S(1)}, f32[2,128,1024]{2,1,0:T(8,128)S(1)}, bf16[4,40,8,128]{3,2,1,0:T(8,128)(2,1)S(1)}) custom-call(bf16[128,512]{1,0:T(8,128)(2,1)S(1)} %bitcast.14, bf16[128,10240]{1,0:T(8,128)(2,1)} %g_hbm.1, bf16[2,128,1024]{2,1,0:T(8,128)(2,1)S(1)} %bitcast.15, bf16[2,1024,1024]{2,1,0:T(8,128)(2,1)} %bitcast.17, ...), custom_call_target="tpu_custom_call" | custom-call | flops 4000000000 | bytes 16000000 | tf_op jit(solution)/shard_map/pallas_call | solution.py:546
  93.1 0.0 copy-done.1
  93.1 0.0 copy-done.2
  93.1 1.8 %bitcast_add_fusion = (f32[1,2,128,1024]{3,2,1,0:T(8,128)}, f32[1,2,128,1024]{3,2,1,0:T(8,128)}) fusion(f32[2,128,1024]{2,1,0:T(8,128)S(1)} %get-tuple-element.7, f32[1,2,128,1024]{3,2,1,0:T(8,128)S(1)} %copy-done.1, f32[2,128,1024]{2,1,0:T(8,128)S(1)} %get-tuple-element.6, f32[1,2,128,1024]{3,2,1,0:T(8,128)S(1)} %copy-done.2), kind=kLoop, calls=%fused_computation | loop fusion | flops 1572864 | bytes 6291456 | tf_op jit(solution)/shard_map/add | solution.py:607
  94.9 0.8 reshape.16
Async XLA Ops:
  2.2 1.0 %copy-start = (bf16[1,2,128,1024]{3,2,1,0:T(8,128)(2,1)S(1)}, bf16[1,2,128,1024]{3,2,1,0:T(8,128)(2,1)}, u32[]{:S(2)}) copy-start(bf16[1,2,128,1024]{3,2,1,0:T(8,128)(2,1)} %param.12) | copy-start | bytes 1572868
  3.3 89.8 %copy-start.1 = (f32[1,2,128,1024]{3,2,1,0:T(8,128)S(1)}, f32[1,2,128,1024]{3,2,1,0:T(8,128)}, u32[]{:S(2)}) copy-start(f32[1,2,128,1024]{3,2,1,0:T(8,128)} %param.11) | copy-start | bytes 3145732
  3.3 89.8 %copy-start.2 = (f32[1,2,128,1024]{3,2,1,0:T(8,128)S(1)}, f32[1,2,128,1024]{3,2,1,0:T(8,128)}, u32[]{:S(2)}) copy-start(f32[1,2,128,1024]{3,2,1,0:T(8,128)} %param.10) | copy-start | bytes 3145732
